TPU v7x, 512 devices: a whole 4x4x16 slice. The times are simulated.
512 devices in a mesh: row: 16 (over z_hi, y), col: 32 (over z_lo, x, core).
Axes of the slice: x: 4, y: 4, z: 16 (z_hi: 4, z_lo: 4; z = z_hi * 4 + z_lo), core: 2. Of those that a mesh axis runs over, the one named last changes fastest.
Arguments:
- features: bfloat16 [16, 32, 128, 128], P('row', 'col'), may hold values from -6 to 6
- adjacency: bfloat16 [16, 32, 128, 128, 128], P('row', 'col'), may hold values from -0.059814453 to 0.059814453
- block_rows: int32 [16, 32, 128], P('row', 'col'), may hold values from 0 to 31
- block_cols: int32 [16, 32, 128], P('row', 'col'), may hold values from 0 to 15
- counts: int32 [16, 32], P('row', 'col'), may hold values from 32 to 128, as said below
- weights: bfloat16 [2, 128, 128], replicated, may hold values from -0.5 to 0.5
Outputs:
- embedded: bfloat16 [16, 32, 128, 128], P('row', 'col')
Inputs may be any that keep to these rules, and one draw needn't show every extreme that they name: Slots from counts on are unused; some tile uses all 128 slots.
All inputs are finite; a program needn't handle non-finite values.
Results may differ from a plain program's by a relative error of at most 0.009.
Values may be sent and summed in bfloat16 or wider, within the bound.
A program may use at most 64 MiB of HBM per device.

v0:
```python
import jax
import jax.numpy as jnp
from jax import lax
from jax.sharding import PartitionSpec as P

LAYERS = 2


def select_sum(selector, products):
    return jnp.dot(selector, products, precision=lax.Precision.HIGHEST)


def shards(features, adjacency, block_rows, block_cols, counts, weights):
    col_count = lax.axis_size("col")
    blocks = adjacency[0, 0]
    slot_count = blocks.shape[0]
    block_size = blocks.shape[1]
    feat_width = features.shape[-1]
    live_slots = jnp.arange(slot_count, dtype=jnp.int32) < counts[0, 0]
    row_hot = (
        (block_rows[0, 0][None, :] == jnp.arange(col_count, dtype=jnp.int32)[:, None])
        & live_slots[None, :]
    ).astype(jnp.float32)
    targets = block_cols[0, 0]
    current = features[0, 0]
    for layer_index in range(LAYERS):
        gathered = lax.all_gather(current, "row", axis=0, tiled=True)
        picked = gathered.reshape(-1, block_size, feat_width)[targets]
        products = jnp.einsum(
            "kij,kjf->kif", blocks, picked, preferred_element_type=jnp.float32
        ).reshape(slot_count, block_size * feat_width)
        partial_value = select_sum(row_hot, products)
        summed = lax.psum_scatter(partial_value, "col", scatter_dimension=0, tiled=True)
        aggregated = summed.reshape(block_size, feat_width).astype(jnp.bfloat16)
        hidden = jnp.dot(aggregated, weights[layer_index], preferred_element_type=jnp.float32)
        if layer_index + 1 < LAYERS:
            hidden = jax.nn.relu(hidden)
        current = hidden.astype(jnp.bfloat16)
    return current[None, None]


def solution(mesh):
    placed = (
        P("row", "col", None, None),
        P("row", "col", None, None, None),
        P("row", "col", None),
        P("row", "col", None),
        P("row", "col"),
        P(),
    )
    return jax.shard_map(
        shards, mesh=mesh, in_specs=placed, out_specs=P("row", "col", None, None), check_vma=False
    )
```

profile of v0, /device:TPU:1, one launch (start us, length us, event | category | flops | bytes accessed | tf_op | source)
XLA Modules:
  0.0 487.6 jit_solution(8775197711665834184)
XLA Ops:
  0.0 0.7 fusion.29
  0.7 57.0 %all-gather = bf16[1,1,2048,128]{3,2,1,0:T(8,128)(2,1)S(1)} all-gather(bf16[1,1,128,128]{3,2,1,0:T(8,128)(2,1)} %param.6), channel_id=2, replica_groups=mesh['row'=16,'col'=32] {'row'}, dimensions={2}, use_global_device_ids=true | all-gather | bytes 557056 | tf_op jit(solution)/shard_map/all_gather | solution.py:27
  57.6 3.1 gather_fusion
  60.7 9.8 %fusion.4 = f32[128,128,128]{1,2,0:T(8,128)} fusion(bf16[128,128,128]{2,1,0:T(8,128)(2,1)} %gather_fusion, bf16[1,1,128,128,128]{4,3,2,1,0:T(8,128)(2,1)} %param.7), kind=kOutput, calls=%fused_computation.6 | convolution fusion | flops 536870912 | bytes 16777216 | tf_op jit(solution)/shard_map/kij,kjf->kif/dot_general | solution.py:29
  70.5 0.0 copy-start.1
  70.5 9.3 %copy.12 = f32[128,128,128]{0,2,1:T(8,128)} copy(f32[128,128,128]{1,2,0:T(8,128)} %fusion.4) | data formatting | bytes 16777216 | tf_op jit(solution)/shard_map/kij,kjf->kif/dot_general | solution.py:29
  80.5 0.0 copy-done.1
  80.5 0.0 copy-start
  80.5 7.0 %fusion.23 = f32[32,16384]{1,0:T(8,128)S(1)} fusion(f32[128,16384]{0,1:T(8,128)} %bitcast.45, s32[128]{0:T(128)S(1)} %bitcast.47, pred[128]{0:T(512)(128)(4,1)S(1)} %iota_compare_fusion.1), kind=kOutput, calls=%fused_computation.25 | convolution fusion | flops 805314560 | bytes 10486400 | tf_op jit(solution)/shard_map/dot_general | solution.py:10
  87.5 162.8 %all-reduce.4 = bf16[32,16384]{1,0:T(8,128)(2,1)S(1)} all-reduce(f32[32,16384]{1,0:T(8,128)S(1)} %fusion.23), channel_id=3, replica_groups=mesh['row'=16,'col'=32] {'col'}, use_global_device_ids=true, to_apply=%region_0.0.clone | all-reduce | flops 524288 | bytes 3145728
  250.3 1.3 dynamic-slice
  251.6 0.9 fusion.13
  252.5 0.0 copy-done
  252.5 0.1 fusion.10
  252.6 43.5 %all_gather.7 = bf16[2048,128]{1,0:T(8,128)(2,1)S(1)} all-gather(bf16[128,128]{1,0:T(8,128)(2,1)S(1)} %fusion.10), channel_id=1, replica_groups=mesh['row'=16,'col'=32] {'row'}, dimensions={0}, use_global_device_ids=true | all-gather | bytes 557056 | tf_op jit(solution)/shard_map/all_gather | solution.py:27
  296.1 3.1 gather_fusion.1
  299.1 9.8 %fusion.7 = f32[128,128,128]{1,2,0:T(8,128)} fusion(bf16[128,128,128]{2,1,0:T(8,128)(2,1)} %gather_fusion.1, bf16[1,1,128,128,128]{4,3,2,1,0:T(8,128)(2,1)} %param.7), kind=kOutput, calls=%fused_computation.7 | convolution fusion | flops 536870912 | bytes 16777216 | tf_op jit(solution)/shard_map/kij,kjf->kif/dot_general | solution.py:29
  308.9 9.3 %copy.14 = f32[128,128,128]{0,2,1:T(8,128)} copy(f32[128,128,128]{1,2,0:T(8,128)} %fusion.7) | data formatting | bytes 16777216 | tf_op jit(solution)/shard_map/kij,kjf->kif/dot_general | solution.py:29
  318.2 7.0 %fusion.21 = f32[32,16384]{1,0:T(8,128)S(1)} fusion(f32[128,16384]{0,1:T(8,128)} %bitcast.46, s32[128]{0:T(128)S(1)} %bitcast.48, pred[128]{0:T(512)(128)(4,1)S(1)} %iota_compare_fusion.1), kind=kOutput, calls=%fused_computation.24 | convolution fusion | flops 805314560 | bytes 10486400 | tf_op jit(solution)/shard_map/dot_general | solution.py:10
  325.2 160.8 %all-reduce.5 = bf16[32,16384]{1,0:T(8,128)(2,1)S(1)} all-reduce(f32[32,16384]{1,0:T(8,128)S(1)} %fusion.21), channel_id=4, replica_groups=mesh['row'=16,'col'=32] {'col'}, use_global_device_ids=true, to_apply=%region_1.2.clone | all-reduce | flops 524288 | bytes 3145728
  486.0 0.9 fusion.12
  486.8 0.8 fusion.11
  (2 shorter events, 0.0 us)
Async XLA Ops:
  70.5 10.0 %copy-start.1 = (s32[1,1,128]{2,1,0:T(1,128)S(1)}, s32[1,1,128]{2,1,0:T(1,128)}, u32[]{:S(2)}) copy-start(s32[1,1,128]{2,1,0:T(1,128)} %param.8) | copy-start | bytes 1540
  80.5 172.0 %copy-start = (bf16[2,128,128]{2,1,0:T(8,128)(2,1)S(1)}, bf16[2,128,128]{2,1,0:T(8,128)(2,1)}, u32[]{:S(2)}) copy-start(bf16[2,128,128]{2,1,0:T(8,128)(2,1)} %param.11) | copy-start | bytes 196612
where the time goes:
time: 492 us; the launch traced here: 488 us
  blocking collectives  424 us (86%)
  matrix products  34.4 us (7%)
  local copies, waits for them, and re-layouts  27.8 us (6%)
    unnamed x2, blocking collectives  324 us
    all_gather x2, blocking collectives, shards(): gathered = lax.all_gather(current, 'row', axis=0, tiled=True)  100 us
    dot_general x2, matrix products, shards(): jnp.einsum('kij,kjf->kif', blocks, picked, preferred_element_type=jnp.flo...  19.5 us
    dot_general x2, local copies, waits for them, and re-layouts, shards(): jnp.einsum('kij,kjf->kif', blocks, picked, preferred_element_type=jnp.flo...  18.7 us
    dot_general x2, matrix products, select_sum(): return jnp.dot(selector, products, precision=lax.Precision.HIGHEST)  14 us

commit v1 on v0

v1 whole, which is shorter than its diff:
```python
import functools

import jax
import jax.numpy as jnp
from jax import lax
from jax.experimental import pallas as pl
from jax.experimental.pallas import tpu as pltpu
from jax.sharding import PartitionSpec as P

LAYERS = 2
BLOCK = 128
HALF = 64
ROWS = 16
PAIRS = 80
UNROLL = 4
DZ_ORDER = (2, 1, 3, 0)
DX_ORDER = (2, 1, 3, 0)
MESH = pl.DeviceIdType.MESH


def turned(vector):
    return jnp.transpose(jnp.broadcast_to(vector, (BLOCK, BLOCK)))


def slot_table(rows, cols, count):
    lane = lax.broadcasted_iota(jnp.int32, (BLOCK, BLOCK), 1)
    sub = lax.broadcasted_iota(jnp.int32, (BLOCK, BLOCK), 0)
    one = lane[:1]
    live = one < count
    rows = jnp.where(live, rows, BLOCK)
    rows_b = jnp.broadcast_to(rows, (BLOCK, BLOCK))
    rows_t = turned(rows)
    rank = jnp.sum(((rows_b == rows_t) & (sub < lane)).astype(jnp.int32), axis=0, keepdims=True)
    sizes = jnp.sum((rows_t == lane).astype(jnp.int32), axis=0, keepdims=True)
    pairs = turned((sizes + 1) >> 1)
    firsts = jnp.sum(jnp.where(sub < lane, pairs, 0), axis=0, keepdims=True)
    before = jnp.sum(jnp.where(sub < rows_b, pairs, 0), axis=0, keepdims=True)
    place = jnp.where(live, 2 * before + rank, 4 * BLOCK)
    packed = turned(place * 4096 + cols * BLOCK + one)
    place_t = packed >> 12
    value = (packed & 4095) - ROWS * BLOCK
    tables = [
        jnp.sum(jnp.where(place_t == lane + base, value, 0), axis=0, keepdims=True) + ROWS * BLOCK
        for base in (0, BLOCK)
    ]
    return firsts, tables[0], tables[1]


def kernel(
    feat_hbm, adj_hbm, rows_hbm, cols_hbm, count_hbm, weight_hbm, out_ref,
    adj, rows_v, cols_v, count_v, weight_v, held_0, held_1, prefix, table_v, table_s,
    send_c, recv_c, send_x, recv_x, send_m, recv_m, send_z, recv_z,
    local_sem, gs_sem, gr_sem, cs_sem, cr_sem, xs_sem, xr_sem, ms_sem, mr_sem, zs_sem, zr_sem,
):
    row, col = lax.axis_index("row"), lax.axis_index("col")
    zh, y = row // 4, row % 4
    zl, x, core = col // 8, (col // 2) % 4, col % 2

    def at_row(dz, dy):
        return ((zh + dz) % 4) * 4 + (y + dy) % 4

    def at_col(dz, dx, other):
        side = 1 - core if other else core
        return ((zl + dz) % 4) * 8 + ((x + dx) % 4) * 2 + side

    z_up, z_down = (at_row(1, 0), col), (at_row(3, 0), col)
    y_up, y_down = (at_row(0, 1), col), (at_row(0, 3), col)
    sibling = (row, at_col(0, 0, True))
    x_up, x_down = (row, at_col(0, 1, False)), (row, at_col(0, 3, False))
    peers = {dz: (row, at_col(dz, 0, False)) for dz in (1, 2, 3)}

    helds = (held_0, held_1)
    loads = [
        pltpu.make_async_copy(source, target, local_sem.at[at])
        for at, (source, target) in enumerate((
            (rows_hbm, rows_v), (cols_hbm, cols_v), (count_hbm, count_v),
            (feat_hbm, held_0.at[row]), (weight_hbm, weight_v), (adj_hbm, adj),
        ))
    ]
    for load in loads:
        load.start()

    barrier = pltpu.get_barrier_semaphore()
    partners = [z_up, z_down, y_up, y_down, sibling, x_up, x_down] + list(peers.values())
    for partner in partners:
        pl.semaphore_signal(barrier, inc=1, device_id=partner, device_id_type=MESH)
    for held in helds:
        held[ROWS] = jnp.zeros((BLOCK, BLOCK), jnp.bfloat16)
    prefix[0] = jnp.zeros((BLOCK, BLOCK), jnp.float32)
    pl.semaphore_wait(barrier, len(partners))

    sent = []

    def push(src, dst, send_sem, recv_sem, device):
        copy = pltpu.make_async_remote_copy(
            src_ref=src, dst_ref=dst, send_sem=send_sem, recv_sem=recv_sem,
            device_id=device, device_id_type=MESH,
        )
        copy.start()
        sent.append(copy)

    def await_into(dst, recv_sem):
        pltpu.make_async_remote_copy(
            src_ref=dst, dst_ref=dst, send_sem=recv_sem, recv_sem=recv_sem,
            device_id=sibling, device_id_type=MESH,
        ).wait_recv()

    for layer in range(LAYERS):
        count = [0]
        held = helds[layer]

        def half_of(origin, half):
            return held.at[origin, pl.ds(half * HALF, HALF)]

        def give(dz, dy, half, device):
            origin = at_row(dz, dy)
            source = half_of(origin, half)
            if layer == 0 and dz == 0 and dy == 0:
                source = feat_hbm.at[pl.ds(half * HALF, HALF)]
            push(
                source, half_of(origin, half),
                gs_sem.at[layer, count[0]], gr_sem.at[layer, 2 * origin + half], device,
            )
            count[0] += 1

        def take(dz, dy, half):
            origin = at_row(dz, dy)
            await_into(half_of(origin, half), gr_sem.at[layer, 2 * origin + half])

        def spread(dz, half):
            give(dz, 0, half, y_up if half == 0 else y_down)
            give(dz, 0, half, y_down if half == 0 else y_up)

        def relay_y(dz):
            take(dz, 3, 0)
            give(dz, 3, 0, y_up)
            take(dz, 1, 1)
            give(dz, 1, 1, y_down)

        give(0, 0, 0, z_up)
        give(0, 0, 1, z_down)
        give(0, 0, 1, z_up)
        give(0, 0, 0, z_down)
        spread(0, 0)
        spread(0, 1)

        if layer == 0:
            for load in loads[:3]:
                load.wait()
            firsts, low, high = slot_table(rows_v[...], cols_v[...], count_v[...])
            table_v[0:1] = firsts
            table_v[1:2] = low
            table_v[2:3] = high
            to_scalar = pltpu.make_async_copy(table_v, table_s, local_sem.at[6])
            to_scalar.start()

        relay_y(0)
        take(3, 0, 0)
        give(3, 0, 0, z_up)
        take(1, 0, 1)
        give(1, 0, 1, z_down)
        spread(3, 0)
        spread(1, 1)
        take(3, 0, 1)
        spread(3, 1)
        take(1, 0, 0)
        spread(1, 0)
        relay_y(3)
        relay_y(1)
        take(2, 0, 0)
        spread(2, 0)
        take(2, 0, 1)
        spread(2, 1)
        relay_y(2)
        for dz in (0, 3, 1, 2):
            take(dz, 3, 1)
            take(dz, 1, 0)
            take(dz, 2, 0)
            take(dz, 2, 1)

        if layer == 0:
            to_scalar.wait()
            for load in loads[3:]:
                load.wait()

        def pair_step(step, total):
            for part in range(UNROLL):
                pair = step * UNROLL + part
                line = 1 + pair // 64
                first = table_s[line, (2 * pair) % BLOCK]
                second = table_s[line, (2 * pair) % BLOCK + 1]
                left = jnp.concatenate([adj[first & 127], adj[second & 127]], axis=1)
                right = jnp.concatenate([held[first >> 7], held[second >> 7]], axis=0)
                total = total + jnp.dot(left, right, preferred_element_type=jnp.float32)
                prefix[pair + 1] = total
            return total

        lax.fori_loop(0, PAIRS // UNROLL, pair_step, jnp.zeros((BLOCK, BLOCK), jnp.float32))

        def partial(dz, dx, other, low=0, size=BLOCK):
            index = at_col(dz, dx, other)
            first, last = table_s[0, index], table_s[0, index + 1]
            span = pl.ds(low, size)
            return prefix[last, span] - prefix[first, span]

        def own(dz, dx, low=0, size=BLOCK):
            from_sibling = recv_c[layer, dz, dx, pl.ds(low, size)].astype(jnp.float32)
            return partial(dz, dx, False, low, size) + from_sibling

        def stage_core(dz):
            for dx in DX_ORDER:
                send_c[layer, dz, dx] = partial(dz, dx, True).astype(jnp.bfloat16)
            push(
                send_c.at[layer, dz], recv_c.at[layer, dz],
                cs_sem.at[layer, dz], cr_sem.at[layer, dz], sibling,
            )

        def stage_far(dz):
            await_into(recv_c.at[layer, dz], cr_sem.at[layer, dz])
            across = own(dz, 2).astype(jnp.bfloat16)
            send_x[layer, dz, 0, 0:HALF] = across[:HALF]
            send_x[layer, dz, 1, 0:HALF] = across[HALF:]
            send_x[layer, dz, 0, HALF:BLOCK] = own(dz, 1, HALF, HALF).astype(jnp.bfloat16)
            send_x[layer, dz, 1, HALF:BLOCK] = own(dz, 3, 0, HALF).astype(jnp.bfloat16)
            for way, device in ((0, x_up), (1, x_down)):
                push(
                    send_x.at[layer, dz, way], recv_x.at[layer, dz, way],
                    xs_sem.at[layer, dz, way], xr_sem.at[layer, dz, way], device,
                )

        def stage_near(dz):
            for way, dx, low, device in ((0, 1, 0, x_up), (1, 3, HALF, x_down)):
                await_into(recv_x.at[layer, dz, way], xr_sem.at[layer, dz, way])
                relayed = recv_x[layer, dz, way, 0:HALF].astype(jnp.float32)
                send_m[layer, dz, way] = (own(dz, dx, low, HALF) + relayed).astype(jnp.bfloat16)
                push(
                    send_m.at[layer, dz, way], recv_m.at[layer, dz, way],
                    ms_sem.at[layer, dz, way], mr_sem.at[layer, dz, way], device,
                )

        def stage_mine(dz):
            halves = []
            for way, low in ((0, 0), (1, HALF)):
                await_into(recv_m.at[layer, dz, way], mr_sem.at[layer, dz, way])
                merged = recv_m[layer, dz, way].astype(jnp.float32)
                direct = recv_x[layer, dz, 1 - way, HALF:BLOCK].astype(jnp.float32)
                halves.append(own(dz, 0, low, HALF) + merged + direct)
            whole = jnp.concatenate(halves, axis=0)
            if dz == 0:
                return whole
            send_z[layer, dz - 1] = whole.astype(jnp.bfloat16)
            push(
                send_z.at[layer, dz - 1], recv_z.at[layer, dz - 1],
                zs_sem.at[layer, dz - 1], zr_sem.at[layer, dz - 1], peers[dz],
            )
            return None

        for dz in DZ_ORDER:
            stage_core(dz)
        summed = None
        for step in range(len(DZ_ORDER) + 2):
            if step < 4:
                stage_far(DZ_ORDER[step])
            if 1 <= step < 5:
                stage_near(DZ_ORDER[step - 1])
            if step >= 2:
                summed = stage_mine(DZ_ORDER[step - 2])
        for dz in DZ_ORDER[:3]:
            await_into(recv_z.at[layer, dz - 1], zr_sem.at[layer, dz - 1])
            summed = summed + recv_z[layer, dz - 1].astype(jnp.float32)
        hidden = jnp.dot(
            summed.astype(jnp.bfloat16), weight_v[layer], preferred_element_type=jnp.float32
        )
        if layer + 1 < LAYERS:
            helds[layer + 1][row] = jnp.maximum(hidden, 0.0).astype(jnp.bfloat16)
        else:
            out_ref[...] = hidden.astype(jnp.bfloat16)

    for copy in sent:
        copy.wait_send()


def shards(features, adjacency, block_rows, block_cols, counts, weights):
    bf16 = jnp.bfloat16
    out = pl.pallas_call(
        kernel,
        out_shape=jax.ShapeDtypeStruct((BLOCK, BLOCK), bf16),
        in_specs=[pl.BlockSpec(memory_space=pltpu.HBM)] * 6,
        out_specs=pl.BlockSpec(memory_space=pltpu.VMEM),
        scratch_shapes=[
            pltpu.VMEM((BLOCK, BLOCK, BLOCK), bf16),
            pltpu.VMEM((1, BLOCK), jnp.int32),
            pltpu.VMEM((1, BLOCK), jnp.int32),
            pltpu.VMEM((1, 1), jnp.int32),
            pltpu.VMEM((LAYERS, BLOCK, BLOCK), bf16),
            pltpu.VMEM((ROWS + 1, BLOCK, BLOCK), bf16),
            pltpu.VMEM((ROWS + 1, BLOCK, BLOCK), bf16),
            pltpu.VMEM((PAIRS + 1, BLOCK, BLOCK), jnp.float32),
            pltpu.VMEM((8, BLOCK), jnp.int32),
            pltpu.SMEM((8, BLOCK), jnp.int32),
            pltpu.VMEM((LAYERS, 4, 4, BLOCK, BLOCK), bf16),
            pltpu.VMEM((LAYERS, 4, 4, BLOCK, BLOCK), bf16),
            pltpu.VMEM((LAYERS, 4, 2, BLOCK, BLOCK), bf16),
            pltpu.VMEM((LAYERS, 4, 2, BLOCK, BLOCK), bf16),
            pltpu.VMEM((LAYERS, 4, 2, HALF, BLOCK), bf16),
            pltpu.VMEM((LAYERS, 4, 2, HALF, BLOCK), bf16),
            pltpu.VMEM((LAYERS, 3, BLOCK, BLOCK), bf16),
            pltpu.VMEM((LAYERS, 3, BLOCK, BLOCK), bf16),
            pltpu.SemaphoreType.DMA((7,)),
            pltpu.SemaphoreType.DMA((LAYERS, 30)),
            pltpu.SemaphoreType.DMA((LAYERS, 2 * ROWS)),
            pltpu.SemaphoreType.DMA((LAYERS, 4)),
            pltpu.SemaphoreType.DMA((LAYERS, 4)),
            pltpu.SemaphoreType.DMA((LAYERS, 4, 2)),
            pltpu.SemaphoreType.DMA((LAYERS, 4, 2)),
            pltpu.SemaphoreType.DMA((LAYERS, 4, 2)),
            pltpu.SemaphoreType.DMA((LAYERS, 4, 2)),
            pltpu.SemaphoreType.DMA((LAYERS, 3)),
            pltpu.SemaphoreType.DMA((LAYERS, 3)),
        ],
        compiler_params=pltpu.CompilerParams(
            collective_id=0, has_side_effects=True, vmem_limit_bytes=63 * 1024 * 1024
        ),
        cost_estimate=pl.CostEstimate(
            flops=2 * LAYERS * 2 * BLOCK**4, bytes_accessed=2 * BLOCK**3, transcendentals=0
        ),
    )(features[0, 0], adjacency[0, 0], block_rows[0], block_cols[0], counts, weights)
    return out[None, None]


def solution(mesh):
    placed = (
        P("row", "col", None, None),
        P("row", "col", None, None, None),
        P("row", "col", None),
        P("row", "col", None),
        P("row", "col"),
        P(),
    )
    return jax.shard_map(
        shards, mesh=mesh, in_specs=placed, out_specs=P("row", "col", None, None), check_vma=False
    )
```

time: 492 us -> 89.5 us (0.18)
  blocking collectives: 424 us -> 0 us
  Pallas kernels: 0 us -> 87.3 us
  matrix products: 34.4 us -> 0 us
  local copies, waits for them, and re-layouts: 27.8 us -> 1.38 us
    unnamed x2 -> x0, blocking collectives: 324 us -> none
    all_gather x2 -> x0, blocking collectives: 100 us -> none  [shards(): gathered = lax.all_gather(current, 'row', axis=0, tiled=True)]
    pallas_call x0 -> x1, Pallas kernels: none -> 87.3 us  [shards(): pl.pallas_call(kernel, out_shape=jax.ShapeDtypeStruct((BLOCK, BLOCK), bf1...]
    dot_general x6 -> x0, matrix products: 34.4 us -> none  [the longest x2 19.5 us: shards(): jnp.einsum('kij,kjf->kif', blocks, picked, preferred_element_type=jnp.flo...]
    dot_general x2 -> x0, local copies, waits for them, and re-layouts: 18.7 us -> none  [shards(): jnp.einsum('kij,kjf->kif', blocks, picked, preferred_element_type=jnp.flo...]
    gather x2 -> x0, local copies, waits for them, and re-layouts: 6.12 us -> none  [shards(): picked = gathered.reshape(-1, block_size, feat_width)[targets]]
where the time goes in v1:
time: 89.5 us; the launch traced here: 89.3 us
  Pallas kernels  87.3 us (98%)
  local copies, waits for them, and re-layouts  1.38 us (2%)
    pallas_call x1, Pallas kernels, shards(): pl.pallas_call(kernel, out_shape=jax.ShapeDtypeStruct((BLOCK, BLOCK), bf1...  87.3 us

profile of v1, /device:TPU:1, one launch (start us, length us, event | category | flops | bytes accessed | tf_op | source)
XLA Modules:
  0.0 89.3 jit_solution(7929020246005859665)
XLA Ops:
  0.7 87.3 %shard_map.64 = bf16[128,128]{1,0:T(8,128)(2,1)} custom-call(bf16[128,128]{1,0:T(8,128)(2,1)} %bitcast.7, bf16[128,128,128]{2,1,0:T(8,128)(2,1)} %bitcast.6, s32[1,128]{1,0:T(1,128)} %bitcast.8, s32[1,128]{1,0:T(1,128)} %bitcast.9, s32[1,1]{1,0:T(1,128)S(6)} %copy.8.count_hbm, bf16[2,128,128]{2,1,0:T(8,128)(2,1)} %weight_hbm.1), custom_call_target="tpu_custom_call" | custom-call | flops 2147483648 | bytes 4194304 | tf_op jit(solution)/shard_map/pallas_call | solution.py:285
  88.0 1.4 %copy.9 = bf16[1,1,128,128]{3,2,1,0:T(8,128)(2,1)} copy(bf16[1,1,128,128]{3,2,1,0:T(8,128)(2,1)} %bitcast.5) | data formatting | bytes 65536

commit v2 on v0

v2 whole, which is shorter than its diff:
```python
import functools

import jax
import jax.numpy as jnp
from jax import lax
from jax.experimental import pallas as pl
from jax.experimental.pallas import tpu as pltpu
from jax.sharding import PartitionSpec as P

LAYERS = 2
BLOCK = 128
HALF = 64
ROWS = 16
PAIRS = 80
DZ_ORDER = (2, 1, 3, 0)
DX_ORDER = (2, 1, 3, 0)
CHUNKS = [(half, dz) for half in (0, 1) for dz in (2, 1, 3)] + [(0, 0), (1, 0)]
MESH = pl.DeviceIdType.MESH


def turned(vector):
    return jnp.transpose(jnp.broadcast_to(vector, (BLOCK, BLOCK)))


def slot_table(rows, cols, count):
    lane = lax.broadcasted_iota(jnp.int32, (BLOCK, BLOCK), 1)
    sub = lax.broadcasted_iota(jnp.int32, (BLOCK, BLOCK), 0)
    one = lane[:1]
    live = one < count
    rows = jnp.where(live, rows, BLOCK)
    rows_b = jnp.broadcast_to(rows, (BLOCK, BLOCK))
    rows_t = turned(rows)
    rank = jnp.sum(((rows_b == rows_t) & (sub < lane)).astype(jnp.int32), axis=0, keepdims=True)
    sizes = jnp.sum((rows_t == lane).astype(jnp.int32), axis=0, keepdims=True)
    pairs = turned((sizes + 1) >> 1)
    firsts = jnp.sum(jnp.where(sub < lane, pairs, 0), axis=0, keepdims=True)
    before = jnp.sum(jnp.where(sub < rows_b, pairs, 0), axis=0, keepdims=True)
    place = jnp.where(live, 2 * before + rank, 4 * BLOCK)
    packed = turned(place * 4096 + cols * BLOCK + one)
    place_t = packed >> 12
    value = (packed & 4095) - ROWS * BLOCK
    tables = [
        jnp.sum(jnp.where(place_t == lane + base, value, 0), axis=0, keepdims=True) + ROWS * BLOCK
        for base in (0, BLOCK)
    ]
    return firsts, tables[0], tables[1]


def kernel(
    feat_hbm, adj_hbm, rows_hbm, cols_hbm, count_hbm, weight_hbm, out_ref,
    adj, rows_v, cols_v, count_v, weight_v, held_0, held_1, prefix, table_v, table_s,
    send_c, recv_c, send_x, recv_x, send_z, recv_z,
    local_sem, gs_sem, gr_sem, cs_sem, cr_sem, xs_sem, xr_sem, zs_sem, zr_sem,
):
    row, col = lax.axis_index("row"), lax.axis_index("col")
    zh, y = row // 4, row % 4
    zl, x, core = col // 8, (col // 2) % 4, col % 2

    def at_row(dz, dy):
        return ((zh + dz) % 4) * 4 + (y + dy) % 4

    def at_col(dz, dx, other):
        side = 1 - core if other else core
        return ((zl + dz) % 4) * 8 + ((x + dx) % 4) * 2 + side

    z_up, z_down = (at_row(1, 0), col), (at_row(3, 0), col)
    z_across = (at_row(2, 0), col)
    y_peers = {dy: (at_row(0, dy), col) for dy in (1, 2, 3)}
    sibling = (row, at_col(0, 0, True))
    peers = {
        (dz, dx): (row, at_col(dz, dx, False))
        for dz in range(4) for dx in range(4) if (dz, dx) != (0, 0)
    }

    helds = (held_0, held_1)
    loads = [
        pltpu.make_async_copy(source, target, local_sem.at[at])
        for at, (source, target) in enumerate((
            (rows_hbm, rows_v), (cols_hbm, cols_v), (count_hbm, count_v),
            (feat_hbm, held_0.at[row]), (weight_hbm, weight_v), (adj_hbm, adj),
        ))
    ]
    barrier = pltpu.get_barrier_semaphore()
    partners = [z_up, z_down, *y_peers.values(), *peers.values(), sibling]
    for partner in partners:
        pl.semaphore_signal(barrier, inc=1, device_id=partner, device_id_type=MESH)
    for load in loads:
        load.start()
    for held in helds:
        held[ROWS] = jnp.zeros((BLOCK, BLOCK), jnp.bfloat16)
    prefix[0] = jnp.zeros((BLOCK, BLOCK), jnp.float32)
    pl.semaphore_wait(barrier, len(partners))

    sent = []

    def push(src, dst, send_sem, recv_sem, device):
        copy = pltpu.make_async_remote_copy(
            src_ref=src, dst_ref=dst, send_sem=send_sem, recv_sem=recv_sem,
            device_id=device, device_id_type=MESH,
        )
        copy.start()
        sent.append(copy)

    def await_into(dst, recv_sem):
        pltpu.make_async_remote_copy(
            src_ref=dst, dst_ref=dst, send_sem=recv_sem, recv_sem=recv_sem,
            device_id=sibling, device_id_type=MESH,
        ).wait_recv()

    to_scalar = pltpu.make_async_copy(table_v, table_s, local_sem.at[6])

    def sort_slots():
        for load in loads[:3]:
            load.wait()
        firsts, low, high = slot_table(rows_v[...], cols_v[...], count_v[...])
        table_v[0:1] = firsts
        table_v[1:2] = low
        table_v[2:3] = high
        to_scalar.start()

    given = [0] * LAYERS

    def half_of(layer, origin, half):
        return helds[layer].at[origin, pl.ds(half * HALF, HALF)]

    def give(layer, dz, dy, half, device):
        origin = at_row(dz, dy)
        source = half_of(layer, origin, half)
        if layer == 0 and dz == 0 and dy == 0:
            source = feat_hbm.at[pl.ds(half * HALF, HALF)]
        push(
            source, half_of(layer, origin, half),
            gs_sem.at[layer, given[layer]], gr_sem.at[layer, 2 * origin + half], device,
        )
        given[layer] += 1

    def take(layer, dz, dy, half):
        origin = at_row(dz, dy)
        await_into(half_of(layer, origin, half), gr_sem.at[layer, 2 * origin + half])

    def spread(layer, dz, half):
        for dy in (2, 1, 3):
            give(layer, dz, 0, half, y_peers[dy])

    def gather_give(layer, half):
        if layer > 0:
            give(layer, 0, 0, half, z_across)
        ahead, behind = (z_up, z_down) if half == 0 else (z_down, z_up)
        give(layer, 0, 0, half, ahead)
        give(layer, 0, 0, half, behind)
        spread(layer, 0, half)

    def gather_take(layer):
        take(layer, 3, 0, 0)
        if layer == 0:
            give(layer, 3, 0, 0, z_up)
        spread(layer, 3, 0)
        take(layer, 1, 0, 1)
        if layer == 0:
            give(layer, 1, 0, 1, z_down)
        spread(layer, 1, 1)
        take(layer, 1, 0, 0)
        spread(layer, 1, 0)
        take(layer, 3, 0, 1)
        spread(layer, 3, 1)
        for half in (0, 1):
            take(layer, 2, 0, half)
            spread(layer, 2, half)
        for dz in (0, 3, 1, 2):
            for dy in (1, 3, 2):
                for half in (0, 1):
                    take(layer, dz, dy, half)

    def multiply(layer):
        held = helds[layer]
        total = jnp.zeros((BLOCK, BLOCK), jnp.float32)
        for pair in range(PAIRS):
            line, at = 1 + pair // HALF, 2 * pair % BLOCK
            first, second = table_s[line, at], table_s[line, at + 1]
            left = jnp.concatenate([adj[first & 127], adj[second & 127]], axis=1)
            right = jnp.concatenate([held[first >> 7], held[second >> 7]], axis=0)
            total = total + jnp.dot(left, right, preferred_element_type=jnp.float32)
            prefix[pair + 1] = total

    def partial(half, dz, dx, other):
        index = at_col(dz, dx, other)
        span = pl.ds(half * HALF, HALF)
        return prefix[table_s[0, index + 1], span] - prefix[table_s[0, index], span]

    def own(layer, half, dz, dx):
        from_sibling = recv_c[layer, half, dz, dx].astype(jnp.float32)
        return partial(half, dz, dx, False) + from_sibling

    def stage_core(layer, half, dz):
        for dx in DX_ORDER:
            send_c[layer, half, dz, dx] = partial(half, dz, dx, True).astype(jnp.bfloat16)
        at = (layer, half, dz)
        push(send_c.at[at], recv_c.at[at], cs_sem.at[at], cr_sem.at[at], sibling)

    def stage_far(layer, half, dz):
        at = (layer, half, dz)
        await_into(recv_c.at[at], cr_sem.at[at])
        for dx in DX_ORDER:
            if dx == 0 and (half == 0 or dz == 0):
                continue
            at = (layer, half, dz, dx)
            send_x[at] = own(layer, half, dz, dx).astype(jnp.bfloat16)
            device = peers[dz if half == 1 else 0, dx]
            push(send_x.at[at], recv_x.at[at], xs_sem.at[at], xr_sem.at[at], device)

    def collect(layer, half, dz, dx, whole):
        at = (layer, half, dz, dx)
        await_into(recv_x.at[at], xr_sem.at[at])
        return whole + recv_x[at].astype(jnp.float32)

    def stage_mine(layer, dz):
        whole = own(layer, 0, dz, 0)
        for dx in (1, 3, 2):
            whole = collect(layer, 0, dz, dx, whole)
        if dz > 0:
            at = (layer, dz - 1)
            send_z[at] = whole.astype(jnp.bfloat16)
            push(send_z.at[at], recv_z.at[at], zs_sem.at[at], zr_sem.at[at], peers[dz, 0])
        return whole

    def finish(layer, half, whole):
        hidden = jnp.dot(
            whole.astype(jnp.bfloat16), weight_v[layer], preferred_element_type=jnp.float32
        )
        span = pl.ds(half * HALF, HALF)
        if layer + 1 < LAYERS:
            helds[layer + 1][row, span] = jnp.maximum(hidden, 0.0).astype(jnp.bfloat16)
            gather_give(layer + 1, half)
        else:
            out_ref[span] = hidden.astype(jnp.bfloat16)

    for half in (0, 1):
        gather_give(0, half)
    sort_slots()
    for layer in range(LAYERS):
        gather_take(layer)
        if layer == 0:
            to_scalar.wait()
            for load in loads[3:]:
                load.wait()
        multiply(layer)
        for half, dz in CHUNKS:
            stage_core(layer, half, dz)
        for half, dz in CHUNKS:
            stage_far(layer, half, dz)
        for dz in DZ_ORDER:
            upper = stage_mine(layer, dz)
        for dz in DZ_ORDER[:3]:
            at = (layer, dz - 1)
            await_into(recv_z.at[at], zr_sem.at[at])
            upper = upper + recv_z[at].astype(jnp.float32)
        finish(layer, 0, upper)
        lower = own(layer, 1, 0, 0)
        for dz in DZ_ORDER:
            for dx in (1, 3, 2, 0):
                if (dz, dx) != (0, 0):
                    lower = collect(layer, 1, dz, dx, lower)
        finish(layer, 1, lower)

    for copy in sent:
        copy.wait_send()


def shards(features, adjacency, block_rows, block_cols, counts, weights):
    bf16 = jnp.bfloat16
    out = pl.pallas_call(
        kernel,
        out_shape=jax.ShapeDtypeStruct((BLOCK, BLOCK), bf16),
        in_specs=[pl.BlockSpec(memory_space=pltpu.HBM)] * 6,
        out_specs=pl.BlockSpec(memory_space=pltpu.VMEM),
        scratch_shapes=[
            pltpu.VMEM((BLOCK, BLOCK, BLOCK), bf16),
            pltpu.VMEM((1, BLOCK), jnp.int32),
            pltpu.VMEM((1, BLOCK), jnp.int32),
            pltpu.VMEM((1, 1), jnp.int32),
            pltpu.VMEM((LAYERS, BLOCK, BLOCK), bf16),
            pltpu.VMEM((ROWS + 1, BLOCK, BLOCK), bf16),
            pltpu.VMEM((ROWS + 1, BLOCK, BLOCK), bf16),
            pltpu.VMEM((PAIRS + 1, BLOCK, BLOCK), jnp.float32),
            pltpu.VMEM((8, BLOCK), jnp.int32),
            pltpu.SMEM((8, BLOCK), jnp.int32),
            pltpu.VMEM((LAYERS, 2, 4, 4, HALF, BLOCK), bf16),
            pltpu.VMEM((LAYERS, 2, 4, 4, HALF, BLOCK), bf16),
            pltpu.VMEM((LAYERS, 2, 4, 4, HALF, BLOCK), bf16),
            pltpu.VMEM((LAYERS, 2, 4, 4, HALF, BLOCK), bf16),
            pltpu.VMEM((LAYERS, 3, HALF, BLOCK), bf16),
            pltpu.VMEM((LAYERS, 3, HALF, BLOCK), bf16),
            pltpu.SemaphoreType.DMA((7,)),
            pltpu.SemaphoreType.DMA((LAYERS, 34)),
            pltpu.SemaphoreType.DMA((LAYERS, 2 * ROWS)),
            pltpu.SemaphoreType.DMA((LAYERS, 2, 4)),
            pltpu.SemaphoreType.DMA((LAYERS, 2, 4)),
            pltpu.SemaphoreType.DMA((LAYERS, 2, 4, 4)),
            pltpu.SemaphoreType.DMA((LAYERS, 2, 4, 4)),
            pltpu.SemaphoreType.DMA((LAYERS, 3)),
            pltpu.SemaphoreType.DMA((LAYERS, 3)),
        ],
        compiler_params=pltpu.CompilerParams(
            collective_id=0, has_side_effects=True, vmem_limit_bytes=63 * 1024 * 1024
        ),
        cost_estimate=pl.CostEstimate(
            flops=2 * LAYERS * 2 * BLOCK**4, bytes_accessed=2 * BLOCK**3, transcendentals=0
        ),
    )(features[0, 0], adjacency[0, 0], block_rows[0], block_cols[0], counts, weights)
    return out[None, None]


def solution(mesh):
    placed = (
        P("row", "col", None, None),
        P("row", "col", None, None, None),
        P("row", "col", None),
        P("row", "col", None),
        P("row", "col"),
        P(),
    )
    return jax.shard_map(
        shards, mesh=mesh, in_specs=placed, out_specs=P("row", "col", None, None), check_vma=False
    )
```

time: 492 us -> 73.2 us (0.15)
  blocking collectives: 424 us -> 0 us
  Pallas kernels: 0 us -> 71 us
  matrix products: 34.4 us -> 0 us
  local copies, waits for them, and re-layouts: 27.8 us -> 1.38 us
    unnamed x2 -> x0, blocking collectives: 324 us -> none
    all_gather x2 -> x0, blocking collectives: 100 us -> none  [shards(): gathered = lax.all_gather(current, 'row', axis=0, tiled=True)]
    pallas_call x0 -> x1, Pallas kernels: none -> 71 us  [shards(): pl.pallas_call(kernel, out_shape=jax.ShapeDtypeStruct((BLOCK, BLOCK), bf1...]
    dot_general x6 -> x0, matrix products: 34.4 us -> none  [the longest x2 19.5 us: shards(): jnp.einsum('kij,kjf->kif', blocks, picked, preferred_element_type=jnp.flo...]
    dot_general x2 -> x0, local copies, waits for them, and re-layouts: 18.7 us -> none  [shards(): jnp.einsum('kij,kjf->kif', blocks, picked, preferred_element_type=jnp.flo...]
    gather x2 -> x0, local copies, waits for them, and re-layouts: 6.12 us -> none  [shards(): picked = gathered.reshape(-1, block_size, feat_width)[targets]]
where the time goes in v2:
time: 73.2 us; the launch traced here: 73 us
  Pallas kernels  71 us (97%)
  local copies, waits for them, and re-layouts  1.38 us (2%)
    pallas_call x1, Pallas kernels, shards(): pl.pallas_call(kernel, out_shape=jax.ShapeDtypeStruct((BLOCK, BLOCK), bf1...  71 us

profile of v2, /device:TPU:1, one launch (start us, length us, event | category | flops | bytes accessed | tf_op | source)
XLA Modules:
  0.0 73.0 jit_solution(9391925268165915117)
XLA Ops:
  0.7 71.0 %shard_map.64 = bf16[128,128]{1,0:T(8,128)(2,1)} custom-call(bf16[128,128]{1,0:T(8,128)(2,1)} %bitcast.7, bf16[128,128,128]{2,1,0:T(8,128)(2,1)} %bitcast.6, s32[1,128]{1,0:T(1,128)} %bitcast.8, s32[1,128]{1,0:T(1,128)} %bitcast.9, s32[1,1]{1,0:T(1,128)S(6)} %copy.8.count_hbm, bf16[2,128,128]{2,1,0:T(8,128)(2,1)} %weight_hbm.1), custom_call_target="tpu_custom_call" | custom-call | flops 2147483648 | bytes 4194304 | tf_op jit(solution)/shard_map/pallas_call | solution.py:271
  71.6 1.4 %copy.9 = bf16[1,1,128,128]{3,2,1,0:T(8,128)(2,1)} copy(bf16[1,1,128,128]{3,2,1,0:T(8,128)(2,1)} %bitcast.5) | data formatting | bytes 65536

commit v3 on v2

v3 whole, which is shorter than its diff:
```python
import functools

import jax
import jax.numpy as jnp
from jax import lax
from jax.experimental import pallas as pl
from jax.experimental.pallas import tpu as pltpu
from jax.sharding import PartitionSpec as P

LAYERS = 2
BLOCK = 128
HALF = 64
ROWS = 16
SLOTS = 128
COLS = 32
DZ_ORDER = (2, 1, 3, 0)
DX_ORDER = (2, 1, 3, 0)
CHUNKS = [(half, dz) for half in (0, 1) for dz in (2, 1, 3)] + [(0, 0), (1, 0)]
Y_WAIT = (0, 1, 2, 1)
LAST = [((2, 0), (2, 1)), ((2, 2), (2, 3))]
MESH = pl.DeviceIdType.MESH


def turned(vector):
    return jnp.transpose(jnp.broadcast_to(vector, (BLOCK, BLOCK)))


def slot_table(rows, cols, count):
    lane = lax.broadcasted_iota(jnp.int32, (BLOCK, BLOCK), 1)
    sub = lax.broadcasted_iota(jnp.int32, (BLOCK, BLOCK), 0)
    keys = jnp.where(lane[:1] < count, rows * ROWS + cols, 4 * BLOCK)
    keys_t = turned(keys)

    def last(found):
        slot = jnp.max(jnp.where(found, sub, -1), axis=0, keepdims=True)
        return jnp.where(slot < 0, SLOTS, slot)

    lines = [last(keys_t == lane + line * BLOCK) for line in range(4)]
    return lines + [last((keys_t == keys) & (sub < lane))]


def kernel(
    feat_hbm, adj_hbm, rows_hbm, cols_hbm, count_hbm, weight_hbm, out_ref,
    adj, rows_v, cols_v, count_v, weight_v, held_0, held_1, sums, merged, totals, table_v, table_s,
    send_c, recv_c, send_a, recv_a, send_b, recv_b, send_z, recv_z,
    local_sem, sent_sem, gz_sem, gy_sem, cr_sem, ar_sem, br_sem, zr_sem,
):
    row, col = lax.axis_index("row"), lax.axis_index("col")
    zh, y = row // 4, row % 4
    zl, x, core = col // 8, (col // 2) % 4, col % 2

    def at_row(dz, dy):
        return ((zh + dz) % 4) * 4 + (y + dy) % 4

    def at_col(dz, dx, other):
        side = 1 - core if other else core
        return ((zl + dz) % 4) * 8 + ((x + dx) % 4) * 2 + side

    z_up, z_down = (at_row(1, 0), col), (at_row(3, 0), col)
    y_peers = {dy: (at_row(0, dy), col) for dy in (1, 2, 3)}
    sibling = (row, at_col(0, 0, True))
    peers = {
        (dz, dx): (row, at_col(dz, dx, False))
        for dz in range(4) for dx in range(4) if (dz, dx) != (0, 0)
    }

    helds = (held_0, held_1)
    loads = [
        pltpu.make_async_copy(source, target, local_sem.at[at])
        for at, (source, target) in enumerate((
            (rows_hbm, rows_v), (cols_hbm, cols_v), (count_hbm, count_v),
            (feat_hbm, held_0.at[row]), (weight_hbm, weight_v), (adj_hbm, adj),
        ))
    ]
    barrier = pltpu.get_barrier_semaphore()
    partners = [z_up, z_down, *y_peers.values(), *peers.values(), sibling]
    for partner in partners:
        pl.semaphore_signal(barrier, inc=1, device_id=partner, device_id_type=MESH)
    for load in loads:
        load.start()
    sums[SLOTS] = jnp.zeros((BLOCK, BLOCK), jnp.float32)
    merged[SLOTS] = jnp.zeros((BLOCK, BLOCK), jnp.bfloat16)
    pl.semaphore_wait(barrier, len(partners))

    def push(src, dst, send_sem, recv_sem, device):
        pltpu.make_async_remote_copy(
            src_ref=src, dst_ref=dst, send_sem=send_sem, recv_sem=recv_sem,
            device_id=device, device_id_type=MESH,
        ).start()

    def await_into(dst, recv_sem):
        pltpu.make_async_remote_copy(
            src_ref=dst, dst_ref=dst, send_sem=recv_sem, recv_sem=recv_sem,
            device_id=sibling, device_id_type=MESH,
        ).wait_recv()

    to_scalar = pltpu.make_async_copy(table_v, table_s, local_sem.at[6])

    def sort_slots():
        for load in loads[:3]:
            load.wait()
        for line, row_of in enumerate(slot_table(rows_v[...], cols_v[...], count_v[...])):
            table_v[line : line + 1] = row_of
        to_scalar.start()
        to_scalar.wait()
        for load in loads[3:]:
            load.wait()

        def add_slots(step, carry):
            for part in range(8):
                slot = step * 8 + part
                total = adj[slot].astype(jnp.float32) + sums[table_s[4, slot]]
                sums[slot] = total
                merged[slot] = total.astype(jnp.bfloat16)
            return carry

        lax.fori_loop(0, SLOTS // 8, add_slots, 0)

    def half_of(layer, origin, half):
        return helds[layer].at[origin, pl.ds(half * HALF, HALF)]

    def give(layer, dz, half, recv_sem, device):
        origin = at_row(dz, 0)
        target = half_of(layer, origin, half)
        source = target
        if layer == 0 and dz == 0:
            source = feat_hbm.at[pl.ds(half * HALF, HALF)]
        push(source, target, sent_sem.at[layer, 0], recv_sem, device)

    def give_z(layer, dz, half, step):
        away = (dz - step) % 4
        device = (at_row(step, 0), col)
        give(layer, dz, half, gz_sem.at[layer, 2 * (away - 1) + half], device)

    def take_z(layer, dz, half):
        await_into(half_of(layer, at_row(dz, 0), half), gz_sem.at[layer, 2 * (dz - 1) + half])

    def spread(layer, dz, half):
        for dy in (2, 1, 3):
            give(layer, dz, half, gy_sem.at[layer, Y_WAIT[dz]], y_peers[dy])

    def take_y(layer, wait, blocks):
        await_into(helds[layer].at[pl.ds(0, blocks)], gy_sem.at[layer, wait])

    def gather_give(layer, half):
        if layer > 0:
            give_z(layer, 0, half, 2)
        ahead = 1 if half == 0 else 3
        give_z(layer, 0, half, ahead)
        give_z(layer, 0, half, 4 - ahead)
        spread(layer, 0, half)

    def gather_take(layer):
        for dz, half, step in ((3, 0, 1), (1, 1, 3), (1, 0, 0), (3, 1, 0)):
            take_z(layer, dz, half)
            if layer == 0 and step > 0:
                give_z(layer, dz, half, step)
            spread(layer, dz, half)
        take_y(layer, 0, 3)
        multiply(layer, [((0, 0), (0, 1)), ((0, 2), (0, 3))], True)
        for half in (0, 1):
            take_z(layer, 2, half)
            spread(layer, 2, half)
        multiply(layer, [((3, 0), (1, 0))], False)
        take_y(layer, 1, 6)
        multiply(layer, [((3, 1), (3, 3)), ((1, 1), (1, 3))], False)
        multiply(layer, [((3, 2), (1, 2))], False)
        take_y(layer, 2, 3)

    def products(layer, groups, block):
        held = helds[layer]
        total = None
        for group in groups:
            origins = [at_row(*step) for step in group]
            slots = [table_s[block // 8, block % 8 * ROWS + origin] for origin in origins]
            left = jnp.concatenate([merged[slot] for slot in slots], axis=1)
            right = jnp.concatenate([held[origin] for origin in origins], axis=0)
            term = jnp.dot(left, right, preferred_element_type=jnp.float32)
            total = term if total is None else total + term
        return total

    def multiply(layer, groups, fresh):
        def step(at, carry):
            for inner in range(16):
                block = at * 16 + inner
                total = products(layer, groups, block)
                totals[block] = total if fresh else totals[block] + total
            return carry

        lax.fori_loop(0, COLS // 16, step, 0)

    def complete(layer, dz, dx, other):
        block = at_col(dz, dx, other)
        return totals[block] + products(layer, LAST, block)

    def own(layer, half, dz, dx):
        from_sibling = recv_c[layer, dz, half, dx].astype(jnp.float32)
        return totals[at_col(dz, dx, False), pl.ds(half * HALF, HALF)] + from_sibling

    def stage_core(layer, dz):
        for dx in DX_ORDER:
            whole = complete(layer, dz, dx, True).astype(jnp.bfloat16)
            send_c[layer, dz, 0, dx] = whole[:HALF]
            send_c[layer, dz, 1, dx] = whole[HALF:]
        at = (layer, dz)
        push(send_c.at[at], recv_c.at[at], sent_sem.at[layer, 1], cr_sem.at[at], sibling)

    def stage_far(layer, half, dz):
        if half == 0:
            await_into(recv_c.at[layer, dz], cr_sem.at[layer, dz])
        for dx in DX_ORDER:
            if half == 0 and dx > 0:
                at = (layer, dz, dx - 1)
                send_a[at] = own(layer, 0, dz, dx).astype(jnp.bfloat16)
                push(
                    send_a.at[at], recv_a.at[at],
                    sent_sem.at[layer, 2], ar_sem.at[layer, dz], peers[0, dx],
                )
            if half == 1 and (dz, dx) != (0, 0):
                at = (layer, 4 * dz + dx - 1)
                send_b[at] = own(layer, 1, dz, dx).astype(jnp.bfloat16)
                push(
                    send_b.at[at], recv_b.at[at],
                    sent_sem.at[layer, 3], br_sem.at[layer], peers[dz, dx],
                )

    def stage_mine(layer, dz):
        await_into(recv_a.at[layer, dz], ar_sem.at[layer, dz])
        whole = own(layer, 0, dz, 0)
        for at in range(3):
            whole = whole + recv_a[layer, dz, at].astype(jnp.float32)
        if dz > 0:
            at = (layer, dz - 1)
            send_z[at] = whole.astype(jnp.bfloat16)
            push(send_z.at[at], recv_z.at[at], sent_sem.at[layer, 4], zr_sem.at[layer], peers[dz, 0])
        return whole

    def finish(layer, half, whole):
        hidden = jnp.dot(
            whole.astype(jnp.bfloat16), weight_v[layer], preferred_element_type=jnp.float32
        )
        span = pl.ds(half * HALF, HALF)
        if layer + 1 < LAYERS:
            helds[layer + 1][row, span] = jnp.maximum(hidden, 0.0).astype(jnp.bfloat16)
            gather_give(layer + 1, half)
        else:
            out_ref[span] = hidden.astype(jnp.bfloat16)

    for half in (0, 1):
        gather_give(0, half)
    sort_slots()
    for layer in range(LAYERS):
        gather_take(layer)
        for dz in DZ_ORDER:
            stage_core(layer, dz)
        for dz in DZ_ORDER:
            for dx in DX_ORDER:
                totals[at_col(dz, dx, False)] = complete(layer, dz, dx, False)
        for half, dz in CHUNKS:
            stage_far(layer, half, dz)
        for dz in DZ_ORDER:
            upper = stage_mine(layer, dz)
        await_into(recv_z.at[layer], zr_sem.at[layer])
        for at in range(3):
            upper = upper + recv_z[layer, at].astype(jnp.float32)
        finish(layer, 0, upper)
        await_into(recv_b.at[layer], br_sem.at[layer])
        lower = own(layer, 1, 0, 0)
        for at in range(15):
            lower = lower + recv_b[layer, at].astype(jnp.float32)
        finish(layer, 1, lower)

    for layer in range(LAYERS):
        sources = (
            helds[layer].at[pl.ds(0, 15)], send_c.at[layer], send_a.at[layer],
            send_b.at[layer], send_z.at[layer],
        )
        for kind, source in enumerate(sources):
            pltpu.make_async_remote_copy(
                src_ref=source, dst_ref=source,
                send_sem=sent_sem.at[layer, kind], recv_sem=sent_sem.at[layer, kind],
                device_id=sibling, device_id_type=MESH,
            ).wait_send()


def shards(features, adjacency, block_rows, block_cols, counts, weights):
    bf16 = jnp.bfloat16
    out = pl.pallas_call(
        kernel,
        out_shape=jax.ShapeDtypeStruct((BLOCK, BLOCK), bf16),
        in_specs=[pl.BlockSpec(memory_space=pltpu.HBM)] * 6,
        out_specs=pl.BlockSpec(memory_space=pltpu.VMEM),
        scratch_shapes=[
            pltpu.VMEM((BLOCK, BLOCK, BLOCK), bf16),
            pltpu.VMEM((1, BLOCK), jnp.int32),
            pltpu.VMEM((1, BLOCK), jnp.int32),
            pltpu.VMEM((1, 1), jnp.int32),
            pltpu.VMEM((LAYERS, BLOCK, BLOCK), bf16),
            pltpu.VMEM((ROWS, BLOCK, BLOCK), bf16),
            pltpu.VMEM((ROWS, BLOCK, BLOCK), bf16),
            pltpu.VMEM((SLOTS + 1, BLOCK, BLOCK), jnp.float32),
            pltpu.VMEM((SLOTS + 1, BLOCK, BLOCK), bf16),
            pltpu.VMEM((COLS, BLOCK, BLOCK), jnp.float32),
            pltpu.VMEM((8, BLOCK), jnp.int32),
            pltpu.SMEM((8, BLOCK), jnp.int32),
            pltpu.VMEM((LAYERS, 4, 2, 4, HALF, BLOCK), bf16),
            pltpu.VMEM((LAYERS, 4, 2, 4, HALF, BLOCK), bf16),
            pltpu.VMEM((LAYERS, 4, 3, HALF, BLOCK), bf16),
            pltpu.VMEM((LAYERS, 4, 3, HALF, BLOCK), bf16),
            pltpu.VMEM((LAYERS, 15, HALF, BLOCK), bf16),
            pltpu.VMEM((LAYERS, 15, HALF, BLOCK), bf16),
            pltpu.VMEM((LAYERS, 3, HALF, BLOCK), bf16),
            pltpu.VMEM((LAYERS, 3, HALF, BLOCK), bf16),
            pltpu.SemaphoreType.DMA((7,)),
            pltpu.SemaphoreType.DMA((LAYERS, 5)),
            pltpu.SemaphoreType.DMA((LAYERS, 6)),
            pltpu.SemaphoreType.DMA((LAYERS, 3)),
            pltpu.SemaphoreType.DMA((LAYERS, 4)),
            pltpu.SemaphoreType.DMA((LAYERS, 4)),
            pltpu.SemaphoreType.DMA((LAYERS,)),
            pltpu.SemaphoreType.DMA((LAYERS,)),
        ],
        compiler_params=pltpu.CompilerParams(
            collective_id=0, has_side_effects=True, vmem_limit_bytes=63 * 1024 * 1024
        ),
        cost_estimate=pl.CostEstimate(
            flops=2 * LAYERS * ROWS * COLS * BLOCK**3, bytes_accessed=2 * BLOCK**3, transcendentals=0
        ),
    )(features[0, 0], adjacency[0, 0], block_rows[0], block_cols[0], counts, weights)
    return out[None, None]


def solution(mesh):
    placed = (
        P("row", "col", None, None),
        P("row", "col", None, None, None),
        P("row", "col", None),
        P("row", "col", None),
        P("row", "col"),
        P(),
    )
    return jax.shard_map(
        shards, mesh=mesh, in_specs=placed, out_specs=P("row", "col", None, None), check_vma=False
    )
```

time: 73.2 us -> 69.3 us (0.947)
  Pallas kernels: 71 us -> 67 us
    pallas_call x1, Pallas kernels: 71 us -> 67 us  [shards(): pl.pallas_call(kernel, out_shape=jax.ShapeDtypeStruct((BLOCK, BLOCK), bf1...]
where the time goes in v3:
time: 69.3 us; the launch traced here: 69 us
  Pallas kernels  67 us (97%)
  local copies, waits for them, and re-layouts  1.38 us (2%)
    pallas_call x1, Pallas kernels, shards(): pl.pallas_call(kernel, out_shape=jax.ShapeDtypeStruct((BLOCK, BLOCK), bf1...  67 us

profile of v3, /device:TPU:1, one launch (start us, length us, event | category | flops | bytes accessed | tf_op | source)
XLA Modules:
  0.0 69.0 jit_solution(17315115442908284775)
XLA Ops:
  0.7 67.0 %shard_map.64 = bf16[128,128]{1,0:T(8,128)(2,1)} custom-call(bf16[128,128]{1,0:T(8,128)(2,1)} %bitcast.7, bf16[128,128,128]{2,1,0:T(8,128)(2,1)} %bitcast.6, s32[1,128]{1,0:T(1,128)} %bitcast.8, s32[1,128]{1,0:T(1,128)} %bitcast.9, s32[1,1]{1,0:T(1,128)S(6)} %copy.8.count_hbm, bf16[2,128,128]{2,1,0:T(8,128)(2,1)} %weight_hbm.1), custom_call_target="tpu_custom_call" | custom-call | flops 4294967296 | bytes 4194304 | tf_op jit(solution)/shard_map/pallas_call | solution.py:288
  67.6 1.4 %copy.9 = bf16[1,1,128,128]{3,2,1,0:T(8,128)(2,1)} copy(bf16[1,1,128,128]{3,2,1,0:T(8,128)(2,1)} %bitcast.5) | data formatting | bytes 65536

commit v4 on v3

--- a/solution.py
+++ b/solution.py
@@ -15,7 +15,11 @@
 COLS = 32
 DZ_ORDER = (2, 1, 3, 0)
 DX_ORDER = (2, 1, 3, 0)
-CHUNKS = [(half, dz) for half in (0, 1) for dz in (2, 1, 3)] + [(0, 0), (1, 0)]
+CHUNKS = [(0, 2), (1, 2), (0, 1), (0, 3), (1, 1), (1, 3), (0, 0), (1, 0)]
+SUMMED = [(0, 2), (1, 2), (0, 1), (0, 3), (0, 0)]
+DIRECT = [0, 1, 3]
+HOLD = True
+ACROSS_LAST = True
 Y_WAIT = (0, 1, 2, 1)
 LAST = [((2, 0), (2, 1)), ((2, 2), (2, 3))]
 MESH = pl.DeviceIdType.MESH
@@ -43,7 +47,7 @@
     feat_hbm, adj_hbm, rows_hbm, cols_hbm, count_hbm, weight_hbm, out_ref,
     adj, rows_v, cols_v, count_v, weight_v, held_0, held_1, sums, merged, totals, table_v, table_s,
     send_c, recv_c, send_a, recv_a, send_b, recv_b, send_z, recv_z,
-    local_sem, sent_sem, gz_sem, gy_sem, cr_sem, ar_sem, br_sem, zr_sem,
+    local_sem, sent_sem, gz_sem, gy_sem, cr_sem, ar_sem, br_sem, zr_sem, entered_sem,
 ):
     row, col = lax.axis_index("row"), lax.axis_index("col")
     zh, y = row // 4, row % 4
@@ -73,7 +77,8 @@
         ))
     ]
     barrier = pltpu.get_barrier_semaphore()
-    partners = [z_up, z_down, *y_peers.values(), *peers.values(), sibling]
+    near = [peers[0, 1], peers[0, 3], peers[1, 0], peers[3, 0]]
+    partners = [z_up, z_down, *near, *y_peers.values(), sibling]
     for partner in partners:
         pl.semaphore_signal(barrier, inc=1, device_id=partner, device_id_type=MESH)
     for load in loads:
@@ -88,11 +93,24 @@
             device_id=device, device_id_type=MESH,
         ).start()
 
+    def tell_near(turn):
+        for device in near:
+            pl.semaphore_signal(entered_sem.at[turn], inc=1, device_id=device, device_id_type=MESH)
+
+    def hear_near(turn):
+        pl.semaphore_wait(entered_sem.at[turn], len(near))
+
     def await_into(dst, recv_sem):
         pltpu.make_async_remote_copy(
             src_ref=dst, dst_ref=dst, send_sem=recv_sem, recv_sem=recv_sem,
             device_id=sibling, device_id_type=MESH,
         ).wait_recv()
+
+    def await_sent(src, send_sem):
+        pltpu.make_async_remote_copy(
+            src_ref=src, dst_ref=src, send_sem=send_sem, recv_sem=send_sem,
+            device_id=sibling, device_id_type=MESH,
+        ).wait_send()
 
     to_scalar = pltpu.make_async_copy(table_v, table_s, local_sem.at[6])
 
@@ -143,12 +161,15 @@
         await_into(helds[layer].at[pl.ds(0, blocks)], gy_sem.at[layer, wait])
 
     def gather_give(layer, half):
-        if layer > 0:
+        if layer > 0 and not ACROSS_LAST:
             give_z(layer, 0, half, 2)
         ahead = 1 if half == 0 else 3
         give_z(layer, 0, half, ahead)
         give_z(layer, 0, half, 4 - ahead)
         spread(layer, 0, half)
+        if layer > 0 and ACROSS_LAST and half == 1:
+            give_z(layer, 0, 0, 2)
+            give_z(layer, 0, 1, 2)
 
     def gather_take(layer):
         for dz, half, step in ((3, 0, 1), (1, 1, 3), (1, 0, 0), (3, 1, 0)):
@@ -156,6 +177,9 @@
             if layer == 0 and step > 0:
                 give_z(layer, dz, half, step)
             spread(layer, dz, half)
+        if layer == 0:
+            hear_near(1)
+            tell_near(2)
         take_y(layer, 0, 3)
         multiply(layer, [((0, 0), (0, 1)), ((0, 2), (0, 3))], True)
         for half in (0, 1):
@@ -163,8 +187,7 @@
             spread(layer, 2, half)
         multiply(layer, [((3, 0), (1, 0))], False)
         take_y(layer, 1, 6)
-        multiply(layer, [((3, 1), (3, 3)), ((1, 1), (1, 3))], False)
-        multiply(layer, [((3, 2), (1, 2))], False)
+        multiply(layer, [((3, 1), (3, 3)), ((1, 1), (1, 3)), ((3, 2), (1, 2))], False)
         take_y(layer, 2, 3)
 
     def products(layer, groups, block):
@@ -206,31 +229,30 @@
         push(send_c.at[at], recv_c.at[at], sent_sem.at[layer, 1], cr_sem.at[at], sibling)
 
     def stage_far(layer, half, dz):
-        if half == 0:
-            await_into(recv_c.at[layer, dz], cr_sem.at[layer, dz])
         for dx in DX_ORDER:
-            if half == 0 and dx > 0:
-                at = (layer, dz, dx - 1)
-                send_a[at] = own(layer, 0, dz, dx).astype(jnp.bfloat16)
-                push(
-                    send_a.at[at], recv_a.at[at],
-                    sent_sem.at[layer, 2], ar_sem.at[layer, dz], peers[0, dx],
-                )
-            if half == 1 and (dz, dx) != (0, 0):
-                at = (layer, 4 * dz + dx - 1)
+            if (half, dz) in SUMMED:
+                if dx > 0:
+                    at = (layer, SUMMED.index((half, dz)))
+                    send_a[*at, dx - 1] = own(layer, half, dz, dx).astype(jnp.bfloat16)
+                    push(
+                        send_a.at[*at, dx - 1], recv_a.at[*at, dx - 1],
+                        sent_sem.at[layer, 5 if at[1] < 2 else 2], ar_sem.at[at], peers[0, dx],
+                    )
+            elif (dz, dx) != (0, 0):
+                at = (layer, 4 * DIRECT.index(dz) + dx - 1)
                 send_b[at] = own(layer, 1, dz, dx).astype(jnp.bfloat16)
                 push(
                     send_b.at[at], recv_b.at[at],
                     sent_sem.at[layer, 3], br_sem.at[layer], peers[dz, dx],
                 )
 
-    def stage_mine(layer, dz):
-        await_into(recv_a.at[layer, dz], ar_sem.at[layer, dz])
-        whole = own(layer, 0, dz, 0)
-        for at in range(3):
-            whole = whole + recv_a[layer, dz, at].astype(jnp.float32)
+    def stage_mine(layer, half, dz):
+        at = (layer, SUMMED.index((half, dz)))
+        await_into(recv_a.at[at], ar_sem.at[at])
+        whole = own(layer, half, dz, 0)
+        for dx in range(3):
+            whole = whole + recv_a[*at, dx].astype(jnp.float32)
         if dz > 0:
-            at = (layer, dz - 1)
             send_z[at] = whole.astype(jnp.bfloat16)
             push(send_z.at[at], recv_z.at[at], sent_sem.at[layer, 4], zr_sem.at[layer], peers[dz, 0])
         return whole
@@ -248,39 +270,47 @@
 
     for half in (0, 1):
         gather_give(0, half)
+    tell_near(0)
     sort_slots()
+    hear_near(0)
+    tell_near(1)
     for layer in range(LAYERS):
         gather_take(layer)
         for dz in DZ_ORDER:
             stage_core(layer, dz)
-        for dz in DZ_ORDER:
-            for dx in DX_ORDER:
-                totals[at_col(dz, dx, False)] = complete(layer, dz, dx, False)
+        if layer == 0:
+            hear_near(2)
         for half, dz in CHUNKS:
+            if half == 0:
+                for dx in DX_ORDER:
+                    totals[at_col(dz, dx, False)] = complete(layer, dz, dx, False)
+                await_into(recv_c.at[layer, dz], cr_sem.at[layer, dz])
+            if HOLD and (half, dz) == (1, 1):
+                await_sent(send_a.at[layer, pl.ds(0, 2)], sent_sem.at[layer, 5])
             stage_far(layer, half, dz)
-        for dz in DZ_ORDER:
-            upper = stage_mine(layer, dz)
+        for half, dz in SUMMED:
+            upper = stage_mine(layer, half, dz)
         await_into(recv_z.at[layer], zr_sem.at[layer])
-        for at in range(3):
-            upper = upper + recv_z[layer, at].astype(jnp.float32)
+        for at, (half, dz) in enumerate(SUMMED):
+            if half == 0 and dz > 0:
+                upper = upper + recv_z[layer, at].astype(jnp.float32)
         finish(layer, 0, upper)
         await_into(recv_b.at[layer], br_sem.at[layer])
         lower = own(layer, 1, 0, 0)
-        for at in range(15):
+        for at in range(11):
             lower = lower + recv_b[layer, at].astype(jnp.float32)
+        lower = lower + recv_z[layer, SUMMED.index((1, 2))].astype(jnp.float32)
         finish(layer, 1, lower)
 
     for layer in range(LAYERS):
-        sources = (
-            helds[layer].at[pl.ds(0, 15)], send_c.at[layer], send_a.at[layer],
+        sources = [
+            helds[layer].at[pl.ds(0, 15)], send_c.at[layer], send_a.at[layer, pl.ds(2, 3)],
             send_b.at[layer], send_z.at[layer],
-        )
+        ]
+        if not HOLD:
+            sources.append(send_a.at[layer, pl.ds(0, 2)])
         for kind, source in enumerate(sources):
-            pltpu.make_async_remote_copy(
-                src_ref=source, dst_ref=source,
-                send_sem=sent_sem.at[layer, kind], recv_sem=sent_sem.at[layer, kind],
-                device_id=sibling, device_id_type=MESH,
-            ).wait_send()
+            await_sent(source, sent_sem.at[layer, kind])
 
 
 def shards(features, adjacency, block_rows, block_cols, counts, weights):
@@ -305,20 +335,21 @@
             pltpu.SMEM((8, BLOCK), jnp.int32),
             pltpu.VMEM((LAYERS, 4, 2, 4, HALF, BLOCK), bf16),
             pltpu.VMEM((LAYERS, 4, 2, 4, HALF, BLOCK), bf16),
-            pltpu.VMEM((LAYERS, 4, 3, HALF, BLOCK), bf16),
-            pltpu.VMEM((LAYERS, 4, 3, HALF, BLOCK), bf16),
-            pltpu.VMEM((LAYERS, 15, HALF, BLOCK), bf16),
-            pltpu.VMEM((LAYERS, 15, HALF, BLOCK), bf16),
-            pltpu.VMEM((LAYERS, 3, HALF, BLOCK), bf16),
-            pltpu.VMEM((LAYERS, 3, HALF, BLOCK), bf16),
+            pltpu.VMEM((LAYERS, 5, 3, HALF, BLOCK), bf16),
+            pltpu.VMEM((LAYERS, 5, 3, HALF, BLOCK), bf16),
+            pltpu.VMEM((LAYERS, 11, HALF, BLOCK), bf16),
+            pltpu.VMEM((LAYERS, 11, HALF, BLOCK), bf16),
+            pltpu.VMEM((LAYERS, 4, HALF, BLOCK), bf16),
+            pltpu.VMEM((LAYERS, 4, HALF, BLOCK), bf16),
             pltpu.SemaphoreType.DMA((7,)),
-            pltpu.SemaphoreType.DMA((LAYERS, 5)),
+            pltpu.SemaphoreType.DMA((LAYERS, 6)),
             pltpu.SemaphoreType.DMA((LAYERS, 6)),
             pltpu.SemaphoreType.DMA((LAYERS, 3)),
             pltpu.SemaphoreType.DMA((LAYERS, 4)),
-            pltpu.SemaphoreType.DMA((LAYERS, 4)),
+            pltpu.SemaphoreType.DMA((LAYERS, 5)),
             pltpu.SemaphoreType.DMA((LAYERS,)),
             pltpu.SemaphoreType.DMA((LAYERS,)),
+            pltpu.SemaphoreType.REGULAR((3,)),
         ],
         compiler_params=pltpu.CompilerParams(
             collective_id=0, has_side_effects=True, vmem_limit_bytes=63 * 1024 * 1024

time: 69.3 us -> 68.2 us (0.984)
  Pallas kernels: 67 us -> 65.7 us
    pallas_call x1, Pallas kernels: 67 us -> 65.7 us  [shards(): pl.pallas_call(kernel, out_shape=jax.ShapeDtypeStruct((BLOCK, BLOCK), bf1...]
where the time goes in v4:
time: 68.2 us; the launch traced here: 67.7 us
  Pallas kernels  65.7 us (96%)
  local copies, waits for them, and re-layouts  1.38 us (2%)
    pallas_call x1, Pallas kernels, shards(): pl.pallas_call(kernel, out_shape=jax.ShapeDtypeStruct((BLOCK, BLOCK), bf1...  65.7 us
    unnamed x1, local copies, waits for them, and re-layouts  1.38 us

profile of v4, /device:TPU:1, one launch (start us, length us, event | category | flops | bytes accessed | tf_op | source)
XLA Modules:
  0.0 67.7 jit_solution(9013509422524200965)
XLA Ops:
  0.7 65.7 %shard_map.64 = bf16[128,128]{1,0:T(8,128)(2,1)} custom-call(bf16[128,128]{1,0:T(8,128)(2,1)} %bitcast.7, bf16[128,128,128]{2,1,0:T(8,128)(2,1)} %bitcast.6, s32[1,128]{1,0:T(1,128)} %bitcast.8, s32[1,128]{1,0:T(1,128)} %bitcast.9, s32[1,1]{1,0:T(1,128)S(6)} %copy.8.count_hbm, bf16[2,128,128]{2,1,0:T(8,128)(2,1)} %weight_hbm.1), custom_call_target="tpu_custom_call" | custom-call | flops 4294967296 | bytes 4194304 | tf_op jit(solution)/shard_map/pallas_call | solution.py:318
  66.3 1.4 %copy.9 = bf16[1,1,128,128]{3,2,1,0:T(8,128)(2,1)} copy(bf16[1,1,128,128]{3,2,1,0:T(8,128)(2,1)} %bitcast.5) | data formatting | bytes 65536

commit v5 on v4

--- a/solution.py
+++ b/solution.py
@@ -18,8 +18,6 @@
 CHUNKS = [(0, 2), (1, 2), (0, 1), (0, 3), (1, 1), (1, 3), (0, 0), (1, 0)]
 SUMMED = [(0, 2), (1, 2), (0, 1), (0, 3), (0, 0)]
 DIRECT = [0, 1, 3]
-HOLD = True
-ACROSS_LAST = True
 Y_WAIT = (0, 1, 2, 1)
 LAST = [((2, 0), (2, 1)), ((2, 2), (2, 3))]
 MESH = pl.DeviceIdType.MESH
@@ -112,6 +110,14 @@
             device_id=sibling, device_id_type=MESH,
         ).wait_send()
 
+    def settle(layer, kinds):
+        sources = (
+            helds[layer].at[pl.ds(0, 15)], send_c.at[layer], send_a.at[layer, pl.ds(2, 3)],
+            send_b.at[layer], send_z.at[layer],
+        )
+        for kind in kinds:
+            await_sent(sources[kind], sent_sem.at[layer, kind])
+
     to_scalar = pltpu.make_async_copy(table_v, table_s, local_sem.at[6])
 
     def sort_slots():
@@ -155,19 +161,18 @@
 
     def spread(layer, dz, half):
         for dy in (2, 1, 3):
-            give(layer, dz, half, gy_sem.at[layer, Y_WAIT[dz]], y_peers[dy])
+            wait = 3 if dz % 2 == 1 and dy == 2 else Y_WAIT[dz]
+            give(layer, dz, half, gy_sem.at[layer, wait], y_peers[dy])
 
     def take_y(layer, wait, blocks):
         await_into(helds[layer].at[pl.ds(0, blocks)], gy_sem.at[layer, wait])
 
     def gather_give(layer, half):
-        if layer > 0 and not ACROSS_LAST:
-            give_z(layer, 0, half, 2)
         ahead = 1 if half == 0 else 3
         give_z(layer, 0, half, ahead)
         give_z(layer, 0, half, 4 - ahead)
         spread(layer, 0, half)
-        if layer > 0 and ACROSS_LAST and half == 1:
+        if layer > 0 and half == 1:
             give_z(layer, 0, 0, 2)
             give_z(layer, 0, 1, 2)
 
@@ -180,14 +185,18 @@
         if layer == 0:
             hear_near(1)
             tell_near(2)
+        else:
+            settle(layer - 1, (3, 4))
         take_y(layer, 0, 3)
         multiply(layer, [((0, 0), (0, 1)), ((0, 2), (0, 3))], True)
         for half in (0, 1):
             take_z(layer, 2, half)
             spread(layer, 2, half)
         multiply(layer, [((3, 0), (1, 0))], False)
-        take_y(layer, 1, 6)
-        multiply(layer, [((3, 1), (3, 3)), ((1, 1), (1, 3)), ((3, 2), (1, 2))], False)
+        take_y(layer, 1, 4)
+        multiply(layer, [((3, 1), (3, 3)), ((1, 1), (1, 3))], False)
+        take_y(layer, 3, 2)
+        multiply(layer, [((3, 2), (1, 2))], False)
         take_y(layer, 2, 3)
 
     def products(layer, groups, block):
@@ -285,11 +294,12 @@
                 for dx in DX_ORDER:
                     totals[at_col(dz, dx, False)] = complete(layer, dz, dx, False)
                 await_into(recv_c.at[layer, dz], cr_sem.at[layer, dz])
-            if HOLD and (half, dz) == (1, 1):
+            if (half, dz) == (1, 1):
                 await_sent(send_a.at[layer, pl.ds(0, 2)], sent_sem.at[layer, 5])
             stage_far(layer, half, dz)
         for half, dz in SUMMED:
             upper = stage_mine(layer, half, dz)
+        settle(layer, (0, 1, 2))
         await_into(recv_z.at[layer], zr_sem.at[layer])
         for at, (half, dz) in enumerate(SUMMED):
             if half == 0 and dz > 0:
@@ -302,15 +312,7 @@
         lower = lower + recv_z[layer, SUMMED.index((1, 2))].astype(jnp.float32)
         finish(layer, 1, lower)
 
-    for layer in range(LAYERS):
-        sources = [
-            helds[layer].at[pl.ds(0, 15)], send_c.at[layer], send_a.at[layer, pl.ds(2, 3)],
-            send_b.at[layer], send_z.at[layer],
-        ]
-        if not HOLD:
-            sources.append(send_a.at[layer, pl.ds(0, 2)])
-        for kind, source in enumerate(sources):
-            await_sent(source, sent_sem.at[layer, kind])
+    settle(LAYERS - 1, (3, 4))
 
 
 def shards(features, adjacency, block_rows, block_cols, counts, weights):
@@ -344,7 +346,7 @@
             pltpu.SemaphoreType.DMA((7,)),
             pltpu.SemaphoreType.DMA((LAYERS, 6)),
             pltpu.SemaphoreType.DMA((LAYERS, 6)),
-            pltpu.SemaphoreType.DMA((LAYERS, 3)),
+            pltpu.SemaphoreType.DMA((LAYERS, 4)),
             pltpu.SemaphoreType.DMA((LAYERS, 4)),
             pltpu.SemaphoreType.DMA((LAYERS, 5)),
             pltpu.SemaphoreType.DMA((LAYERS,)),

time: 68.2 us -> 68.2 us (level)
  no operation moved by 1% of the time
where the time goes in v5:
time: 68.2 us; the launch traced here: 67.6 us
  Pallas kernels  65.6 us (96%)
  local copies, waits for them, and re-layouts  1.38 us (2%)
    pallas_call x1, Pallas kernels, shards(): pl.pallas_call(kernel, out_shape=jax.ShapeDtypeStruct((BLOCK, BLOCK), bf1...  65.6 us
    unnamed x1, local copies, waits for them, and re-layouts  1.38 us

profile of v5, /device:TPU:1, one launch (start us, length us, event | category | flops | bytes accessed | tf_op | source)
XLA Modules:
  0.0 67.6 jit_solution(18282282532555687407)
XLA Ops:
  0.7 65.6 %shard_map.64 = bf16[128,128]{1,0:T(8,128)(2,1)} custom-call(bf16[128,128]{1,0:T(8,128)(2,1)} %bitcast.7, bf16[128,128,128]{2,1,0:T(8,128)(2,1)} %bitcast.6, s32[1,128]{1,0:T(1,128)} %bitcast.8, s32[1,128]{1,0:T(1,128)} %bitcast.9, s32[1,1]{1,0:T(1,128)S(6)} %copy.8.count_hbm, bf16[2,128,128]{2,1,0:T(8,128)(2,1)} %weight_hbm.1), custom_call_target="tpu_custom_call" | custom-call | flops 4294967296 | bytes 4194304 | tf_op jit(solution)/shard_map/pallas_call | solution.py:320
  66.2 1.4 %copy.9 = bf16[1,1,128,128]{3,2,1,0:T(8,128)(2,1)} copy(bf16[1,1,128,128]{3,2,1,0:T(8,128)(2,1)} %bitcast.5) | data formatting | bytes 65536
